TPU v7x, 32 devices: a whole 2x2x4 slice. The times are simulated.
32 devices in a mesh: parts: 2 (over y), own: 4 (over z), sub: 2 (over x), rep: 2 (over core).
Axes of the slice: x: 2, y: 2, z: 4, core: 2. Of those that a mesh axis runs over, the one named last changes fastest.
Arguments:
- density: float32 [256, 256, 256], P(('parts', 'own', 'sub', 'rep')), parts along dimension 0, may hold values from 0 to 1
- tile_coords: int32 [256, 4], P(('parts', 'own', 'sub', 'rep')), parts along dimension 0, may hold values from -1 to 31, as said below
- neighbours: int32 [256, 8], P(('parts', 'own', 'sub', 'rep')), parts along dimension 0, may hold values from -1 to 127, as said below
- rate_constants: float32 [20], P('parts'), parts along dimension 0, may hold values from 0.05 to 0.5, as said below
Outputs:
- density_next: float32 [256, 256, 256], P(('parts', 'own', 'sub', 'rep')), parts along dimension 0
There are 2 independent parts, one for each index of `parts`. A program takes and returns all parts, laid end to end along the dimension named above; each array names one. Nothing has to cross between parts.
Inputs may be any that keep to these rules, and one draw needn't show every extreme that they name: `tile_coords`: slots come in groups of 8, one group a device, ordered by own, then sub, then rep index. The tile (t1, t2, t3, t4) lies on the device with own index t1, sub index t3 // 2 and rep index t4 // 2, and no tile twice. A device's active tiles fill its first slots; the other slots hold -1 in all four entries. Every device holds 1 to 8 active tiles and some device holds 8. `neighbours`: entry (g, 2k) is the slot of the active tile one lower along species k + 1 than slot g's tile, entry (g, 2k + 1) that of the one one higher, for k = 0 to 3; -1 where that tile is not active or slot g is empty. `rate_constants`: entries 0 and 5 lie in [0.05, 0.25], 1 and 6 in [0.05, 0.25], 2 and 7 in [0.05, 0.2], 3 and 8 in [0.05, 0.25], 4 and 9 in [0.1, 0.5].
All inputs are finite; a program needn't handle non-finite values.
Results may differ from a plain program's by a relative error of at most 0.00002.
Values sent between devices are 32-bit elements; how exact they have to be, the bound alone decides.
A program may use at most 128 MiB of HBM per device.

v0:
```python
import math

import jax
import jax.numpy as jnp
from jax import lax
from jax.sharding import PartitionSpec as P

C_DEV = 2
D_DEV = 2
N1 = 512
N2 = 512
N3 = 256
N4 = 256


def padded(cells, sides, width):
    for axis, dim in sides:
        count = lax.axis_size(axis)
        ends = count - 1
        head = lax.slice_in_dim(cells, 0, width, axis=dim)
        tail = lax.slice_in_dim(cells, cells.shape[dim] - width, cells.shape[dim], axis=dim)
        cells = jnp.concatenate(
            [
                lax.ppermute(tail, axis, [(i, (i + 1) % count) for i in range(ends)]),
                cells,
                lax.ppermute(head, axis, [((i + 1) % count, i) for i in range(ends)]),
            ],
            axis=dim,
        )
    return cells


def layers(values, tile_edge):
    slot_count = values.shape[0]
    tile_area = tile_edge * tile_edge
    by_cells = values.reshape(slot_count, tile_area, tile_edge, tile_edge)
    by_rows = values.reshape(slot_count, tile_edge, tile_edge, tile_area)
    return (
        values[:, :tile_edge, :],
        values[:, tile_area - tile_edge :, :],
        by_rows[:, :, 0, :],
        by_rows[:, :, tile_edge - 1, :],
        jnp.swapaxes(by_cells[:, :, 0, :], 1, 2),
        jnp.swapaxes(by_cells[:, :, tile_edge - 1, :], 1, 2),
        jnp.swapaxes(by_cells[:, :, :, 0], 1, 2),
        jnp.swapaxes(by_cells[:, :, :, tile_edge - 1], 1, 2),
    )


def generator(values, face_set, coords, rate_constants, extents):
    tile_area = values.shape[1]
    tile_edge = math.isqrt(tile_area)
    row_index = lax.broadcasted_iota(jnp.int32, (1, tile_area, tile_area), 1)
    col_index = lax.broadcasted_iota(jnp.int32, (1, tile_area, tile_area), 2)
    row_high = row_index // tile_edge
    row_low = row_index % tile_edge
    col_high = col_index // tile_edge
    col_low = col_index % tile_edge
    anchor = (coords * tile_edge).astype(jnp.float32)[:, :, None, None]
    extent_one, extent_two, extent_three, extent_four = extents
    level_one = anchor[:, 0] + row_high.astype(jnp.float32)
    level_two = anchor[:, 1] + row_low.astype(jnp.float32)
    level_three = anchor[:, 2] + col_high.astype(jnp.float32)
    level_four = anchor[:, 3] + col_low.astype(jnp.float32)
    share_one = level_one / extent_one
    share_two = level_two / extent_two
    share_three = level_three / extent_three
    share_four = level_four / extent_four
    below_one = jnp.where(
        row_high == 0, jnp.tile(face_set[0], (1, tile_edge, 1)), jnp.roll(values, tile_edge, axis=1)
    )
    above_one = jnp.where(
        row_high == tile_edge - 1,
        jnp.tile(face_set[1], (1, tile_edge, 1)),
        jnp.roll(values, -tile_edge, axis=1),
    )
    below_two = jnp.where(
        row_low == 0, jnp.repeat(face_set[2], tile_edge, axis=1), jnp.roll(values, 1, axis=1)
    )
    above_two = jnp.where(
        row_low == tile_edge - 1,
        jnp.repeat(face_set[3], tile_edge, axis=1),
        jnp.roll(values, -1, axis=1),
    )
    below_three = jnp.where(
        col_high == 0,
        jnp.tile(jnp.swapaxes(face_set[4], 1, 2), (1, 1, tile_edge)),
        jnp.roll(values, tile_edge, axis=2),
    )
    above_three = jnp.where(
        col_high == tile_edge - 1,
        jnp.tile(jnp.swapaxes(face_set[5], 1, 2), (1, 1, tile_edge)),
        jnp.roll(values, -tile_edge, axis=2),
    )
    below_four = jnp.where(
        col_low == 0,
        jnp.repeat(jnp.swapaxes(face_set[6], 1, 2), tile_edge, axis=2),
        jnp.roll(values, 1, axis=2),
    )
    above_four = jnp.where(
        col_low == tile_edge - 1,
        jnp.repeat(jnp.swapaxes(face_set[7], 1, 2), tile_edge, axis=2),
        jnp.roll(values, -1, axis=2),
    )
    ratio_two = share_two / rate_constants[4]
    ratio_one = share_one / rate_constants[9]
    transcribe_first = rate_constants[0] / (1.0 + ratio_two * ratio_two)
    transcribe_second = rate_constants[5] / (1.0 + ratio_one * ratio_one)
    outflow = (
        transcribe_first
        + rate_constants[1] * share_three
        + rate_constants[2] * share_three
        + rate_constants[3] * share_one
        + transcribe_second
        + rate_constants[6] * share_four
        + rate_constants[7] * share_four
        + rate_constants[8] * share_two
    )
    inflow = (
        transcribe_first * below_three
        + rate_constants[1] * ((level_three + 1.0) / extent_three) * above_three
        + rate_constants[2] * share_three * below_one
        + rate_constants[3] * ((level_one + 1.0) / extent_one) * above_one
        + transcribe_second * below_four
        + rate_constants[6] * ((level_four + 1.0) / extent_four) * above_four
        + rate_constants[7] * share_four * below_two
        + rate_constants[8] * ((level_two + 1.0) / extent_two) * above_two
    )
    return inflow - outflow * values


def neighbour_faces(values, tile_coords, neighbours, tile_edge):
    lower_one, upper_one, lower_two, upper_two, lower_three, upper_three, lower_four, upper_four = (
        layers(values, tile_edge)
    )
    first_rim = padded(jnp.stack([lower_one, upper_one]), (("own", 0),), 1)
    third_rim = padded(jnp.stack([lower_three, upper_three]), (("sub", 0),), 1)
    fourth_rim = padded(jnp.stack([lower_four, upper_four]), (("rep", 0),), 1)
    third_from_low = third_rim[0]
    third_from_high = third_rim[3]
    fourth_from_low = fourth_rim[0]
    fourth_from_high = fourth_rim[3]
    present = neighbours >= 0
    where_slot = jnp.maximum(neighbours, 0) % values.shape[0]

    def select_face(table, column):
        chosen = jnp.take(table, where_slot[:, column], axis=0)
        return jnp.where(present[:, column, None, None], chosen, 0.0)

    third_low = (tile_coords[:, 2] % C_DEV == 0)[:, None, None]
    third_high = (tile_coords[:, 2] % C_DEV == C_DEV - 1)[:, None, None]
    fourth_low = (tile_coords[:, 3] % D_DEV == 0)[:, None, None]
    fourth_high = (tile_coords[:, 3] % D_DEV == D_DEV - 1)[:, None, None]
    return (
        select_face(first_rim[0], 0),
        select_face(first_rim[3], 1),
        select_face(upper_two, 2),
        select_face(lower_two, 3),
        jnp.where(third_low, select_face(third_from_low, 4), select_face(upper_three, 4)),
        jnp.where(third_high, select_face(third_from_high, 5), select_face(lower_three, 5)),
        jnp.where(fourth_low, select_face(fourth_from_low, 6), select_face(upper_four, 6)),
        jnp.where(fourth_high, select_face(fourth_from_high, 7), select_face(lower_four, 7)),
    )


def on_device(density, tile_coords, neighbours, rate_constants):
    tile_area = density.shape[1]
    tile_edge = math.isqrt(tile_area)
    extents = (float(N1), float(N2), float(N3), float(N4))
    active = tile_coords[:, 0] >= 0
    active_mask = active.astype(jnp.float32)[:, None, None]
    initial = density * active_mask

    def derivative(values):
        face_set = neighbour_faces(values, tile_coords, neighbours, tile_edge)
        change = generator(values, face_set, tile_coords, rate_constants, extents)
        return change * active_mask

    rate_one = derivative(initial)
    middle = initial + rate_one
    rate_two = derivative(middle)
    return initial + 0.5 * (rate_one + rate_two)


def solution(mesh):
    in_specs = (
        P(("parts", "own", "sub", "rep"), None, None),
        P(("parts", "own", "sub", "rep"), None),
        P(("parts", "own", "sub", "rep"), None),
        P("parts"),
    )
    out_specs = P(("parts", "own", "sub", "rep"), None, None)
    return jax.shard_map(
        on_device, mesh=mesh, in_specs=in_specs, out_specs=out_specs, check_vma=False
    )
```

profile of v0, /device:TPU:0, one launch (start us, length us, event | category | flops | bytes accessed | tf_op | source)
XLA Modules:
  0.0 234.6 jit_solution(3888697209967268599)
XLA Ops:
  3.4 5.7 %collective-permute-start.2 = (f32[1,8,16,256]{3,2,1,0:T(8,128)}, f32[1,8,16,256]{3,2,1,0:T(8,128)}, u32[]{:S(2)}, u32[]{:S(2)}) collective-permute-start(f32[1,8,16,256]{3,2,1,0:T(8,128)} %get-tuple-element.62), channel_id=1, source_target_pairs={{0,4},{4,8},{8,12},{1,5},{5,9},{9,13},{2,6},{6,10},{10,14},{3,7},{... | collective-permute-start | bytes 393224 | tf_op jit(solution)/shard_map/ppermute | solution.py:24
  15.3 4.3 %collective-permute-start.4 = (f32[1,8,16,256]{3,2,1,0:T(8,128)}, f32[1,8,16,256]{3,2,1,0:T(8,128)}, u32[]{:S(2)}, u32[]{:S(2)}) collective-permute-start(f32[1,8,16,256]{3,2,1,0:T(8,128)} %bitcast.181), channel_id=1, source_target_pairs={{0,1},{2,3},{4,5},{6,7},{8,9},{10,11},{12,13},{14,15},{16,17},{18,... | collective-permute-start | bytes 393224 | tf_op jit(solution)/shard_map/ppermute | solution.py:24
  21.5 4.0 %collective-permute-start = (f32[1,8,16,256]{3,2,1,0:T(8,128)}, f32[1,8,16,256]{3,2,1,0:T(8,128)}, u32[]{:S(2)}, u32[]{:S(2)}) collective-permute-start(f32[1,8,16,256]{3,2,1,0:T(8,128)} %get-tuple-element.58), channel_id=1, source_target_pairs={{0,2},{1,3},{4,6},{5,7},{8,10},{9,11},{12,14},{13,15},{16,18},{17,... | collective-permute-start | bytes 393224 | tf_op jit(solution)/shard_map/ppermute | solution.py:24
  38.6 2.3 fusion.90
  40.8 2.7 %fusion.92 = (f32[8,256,255]{2,1,0:T(8,128)}, f32[8,256,255]{2,1,0:T(8,128)}) fusion(f32[8,256,256]{2,1,0:T(8,128)S(1)} %broadcast_multiply_fusion), kind=kLoop, calls=%fused_computation.269 | loop fusion | bytes 8355840 | tf_op jit(solution)/shard_map/jit(_roll_static)/slice | solution.py:98
  43.6 2.4 %fusion.96 = (f32[8,255,256]{2,1,0:T(8,128)}, f32[8,255,256]{2,1,0:T(8,128)}) fusion(f32[8,256,256]{2,1,0:T(8,128)S(1)} %broadcast_multiply_fusion), kind=kLoop, calls=%fused_computation.273 | loop fusion | bytes 8355840 | tf_op jit(solution)/shard_map/jit(_roll_static)/slice | solution.py:78
  45.9 2.7 %fusion.89 = (f32[8,256,240]{2,1,0:T(8,128)}, f32[8,256,240]{2,1,0:T(8,128)}) fusion(f32[8,256,256]{2,1,0:T(8,128)S(1)} %broadcast_multiply_fusion), kind=kLoop, calls=%fused_computation.266 | loop fusion | bytes 7864320 | tf_op jit(solution)/shard_map/jit(_roll_static)/slice | solution.py:88
  65.0 2.2 gather_fusion.9
  67.2 2.3 gather_fusion.7
  77.7 2.2 gather_fusion.6
  100.5 17.1 %fusion.77 = (f32[8,256,256]{2,1,0:T(8,128)S(1)}, f32[8,256,256]{2,1,0:T(8,128)}) fusion(f32[8]{0:T(128)} %copy-done.2, f32[8,1,256]{2,1,0:T(1,128)S(1)} %get-tuple-element.77, f32[8,255,256]{2,1,0:T(8,128)} %get-tuple-element.79, f32[8,16,256]{2,1,0:T(8,128)} %select_select_fusion.12, pred[256,256]{1,0:T(8,128)(4,1)S(1)} %get-tuple-element.97, ...), kind=kLoop, calls=%fused_computation.255 | loop fusion | flops 37224448 | bytes 33554632 | tf_op jit(solution)/shard_map/add | solution.py:180
  120.3 2.4 %fusion.84 = (f32[8,256,16,1]{1,3,2,0:T(1,128)}, f32[8,256,16,1]{1,3,2,0:T(1,128)}) fusion(f32[8,256,16,16]{1,3,2,0:T(8,128)} %bitcast.194), kind=kLoop, calls=%fused_computation.261 | loop fusion | bytes 524288 | tf_op jit(solution)/shard_map/slice | solution.py:45
  127.6 2.3 fusion.85
  129.9 2.4 %fusion.80 = (f32[8,255,256]{2,1,0:T(8,128)}, f32[8,255,256]{2,1,0:T(8,128)}) fusion(f32[8,256,256]{2,1,0:T(8,128)S(1)} %get-tuple-element.22), kind=kLoop, calls=%fused_computation.257 | loop fusion | bytes 8355840 | tf_op jit(solution)/shard_map/jit(_roll_static)/slice | solution.py:83
  132.3 2.6 %fusion.86 = (f32[8,256,240]{2,1,0:T(8,128)}, f32[8,256,240]{2,1,0:T(8,128)}) fusion(f32[8,256,256]{2,1,0:T(8,128)S(1)} %get-tuple-element.22), kind=kLoop, calls=%fused_computation.263 | loop fusion | bytes 7864320 | tf_op jit(solution)/shard_map/jit(_roll_static)/slice | solution.py:93
  134.9 2.7 %fusion.82 = (f32[8,256,255]{2,1,0:T(8,128)}, f32[8,256,255]{2,1,0:T(8,128)}) fusion(f32[8,256,256]{2,1,0:T(8,128)S(1)} %get-tuple-element.22), kind=kLoop, calls=%fused_computation.259 | loop fusion | bytes 8355840 | tf_op jit(solution)/shard_map/jit(_roll_static)/slice | solution.py:103
  148.5 5.2 %collective-permute-start.8 = (f32[1,8,16,256]{3,2,1,0:T(8,128)}, f32[1,8,16,256]{3,2,1,0:T(8,128)}, u32[]{:S(2)}, u32[]{:S(2)}) collective-permute-start(f32[1,8,16,256]{3,2,1,0:T(8,128)} %get-tuple-element.28), channel_id=1, source_target_pairs={{0,4},{4,8},{8,12},{1,5},{5,9},{9,13},{2,6},{6,10},{10,14},{3,7},{... | collective-permute-start | bytes 393224 | tf_op jit(solution)/shard_map/ppermute | solution.py:24
  171.6 6.5 %collective-permute-start.6 = (f32[1,8,16,256]{3,2,1,0:T(8,128)}, f32[1,8,16,256]{3,2,1,0:T(8,128)}, u32[]{:S(2)}, u32[]{:S(2)}) collective-permute-start(f32[1,8,16,256]{3,2,1,0:T(8,128)} %get-tuple-element.51), channel_id=1, source_target_pairs={{0,2},{1,3},{4,6},{5,7},{8,10},{9,11},{12,14},{13,15},{16,18},{17,... | collective-permute-start | bytes 393224 | tf_op jit(solution)/shard_map/ppermute | solution.py:24
  180.3 2.2 gather_fusion.17
  197.5 2.9 %copy.36 = f32[8,256,256]{2,1,0:T(8,128)} copy(f32[8,256,256]{1,2,0:T(8,128)} %bitcast.188) | data formatting | bytes 4194304 | tf_op jit(solution)/shard_map/tile | solution.py:87
  203.0 2.9 %copy.38 = f32[8,256,256]{2,1,0:T(8,128)} copy(f32[8,256,256]{1,2,0:T(8,128)} %bitcast.189) | data formatting | bytes 4194304 | tf_op jit(solution)/shard_map/tile | solution.py:92
  208.5 2.9 %copy.40 = f32[8,256,256]{2,1,0:T(8,128)} copy(f32[8,256,256]{1,2,0:T(8,128)} %bitcast.190) | data formatting | bytes 4194304 | tf_op jit(solution)/shard_map/reshape | solution.py:102
  214.0 2.9 %copy.39 = f32[8,256,256]{2,1,0:T(8,128)} copy(f32[8,256,256]{1,2,0:T(8,128)} %bitcast.191) | data formatting | bytes 4194304 | tf_op jit(solution)/shard_map/reshape | solution.py:97
  216.9 17.6 %fusion.17 = f32[8,256,256]{2,1,0:T(8,128)} fusion(f32[8,256,256]{2,1,0:T(8,128)} %get-tuple-element.23, f32[8,256,256]{2,1,0:T(8,128)} %copy.36, f32[8,256,240]{2,1,0:T(8,128)} %get-tuple-element.47, f32[8,256,16]{2,1,0:T(8,128)} %get-tuple-element.49, f32[8,256,256]{2,1,0:T(8,128)} %copy.38, f32[8,256,16]{2,1,0:T(8,128)S(1)} %get-tuple-element.48, ...), kind=kLoop, calls=%fused_computation.53 | loop fusion | flops 38273024 | bytes 35651784 | tf_op jit(solution)/shard_map/add | solution.py:182
  (156 shorter events, 126.6 us)
Async XLA Ops:
  3.4 23.4 %copy-start.10 = (s32[8,4]{0,1:T(4,128)S(1)}, s32[8,4]{0,1:T(4,128)}, u32[]{:S(2)}) copy-start(s32[8,4]{0,1:T(4,128)} %param.7) | copy-start | bytes 388
  3.4 24.1 %copy-start.1 = (s32[8,8]{1,0:T(8,128)S(1)}, s32[8,8]{1,0:T(8,128)}, u32[]{:S(2)}) copy-start(s32[8,8]{1,0:T(8,128)} %param.8) | copy-start | bytes 772
  3.4 92.4 %collective-permute-start.2 = (f32[1,8,16,256]{3,2,1,0:T(8,128)}, f32[1,8,16,256]{3,2,1,0:T(8,128)}, u32[]{:S(2)}, u32[]{:S(2)}) collective-permute-start(f32[1,8,16,256]{3,2,1,0:T(8,128)} %get-tuple-element.62), channel_id=1, source_target_pairs={{0,4},{4,8},{8,12},{1,5},{5,9},{9,13},{2,6},{6,10},{10,14},{3,7},{... | collective-permute-start | bytes 393224 | tf_op jit(solution)/shard_map/ppermute | solution.py:24
  13.3 60.6 %collective-permute-start.5 = (f32[1,8,16,256]{3,2,1,0:T(8,128)}, f32[1,8,16,256]{3,2,1,0:T(8,128)}, u32[]{:S(2)}, u32[]{:S(2)}) collective-permute-start(f32[1,8,16,256]{3,2,1,0:T(8,128)} %bitcast.180), channel_id=1, source_target_pairs={{1,0},{3,2},{5,4},{7,6},{9,8},{11,10},{13,12},{15,14},{17,16},{19,... | collective-permute-start | bytes 393224 | tf_op jit(solution)/shard_map/ppermute | solution.py:26
  15.3 62.4 %collective-permute-start.4 = (f32[1,8,16,256]{3,2,1,0:T(8,128)}, f32[1,8,16,256]{3,2,1,0:T(8,128)}, u32[]{:S(2)}, u32[]{:S(2)}) collective-permute-start(f32[1,8,16,256]{3,2,1,0:T(8,128)} %bitcast.181), channel_id=1, source_target_pairs={{0,1},{2,3},{4,5},{6,7},{8,9},{10,11},{12,13},{14,15},{16,17},{18,... | collective-permute-start | bytes 393224 | tf_op jit(solution)/shard_map/ppermute | solution.py:24
  21.5 58.4 %collective-permute-start = (f32[1,8,16,256]{3,2,1,0:T(8,128)}, f32[1,8,16,256]{3,2,1,0:T(8,128)}, u32[]{:S(2)}, u32[]{:S(2)}) collective-permute-start(f32[1,8,16,256]{3,2,1,0:T(8,128)} %get-tuple-element.58), channel_id=1, source_target_pairs={{0,2},{1,3},{4,6},{5,7},{8,10},{9,11},{12,14},{13,15},{16,18},{17,... | collective-permute-start | bytes 393224 | tf_op jit(solution)/shard_map/ppermute | solution.py:24
  25.6 55.9 %collective-permute-start.1 = (f32[1,8,16,256]{3,2,1,0:T(8,128)}, f32[1,8,16,256]{3,2,1,0:T(8,128)}, u32[]{:S(2)}, u32[]{:S(2)}) collective-permute-start(f32[1,8,16,256]{3,2,1,0:T(8,128)} %get-tuple-element.59), channel_id=1, source_target_pairs={{2,0},{3,1},{6,4},{7,5},{10,8},{11,9},{14,12},{15,13},{18,16},{19,... | collective-permute-start | bytes 393224 | tf_op jit(solution)/shard_map/ppermute | solution.py:26
  45.9 8.8 %copy-start = (f32[10]{0:T(128)S(1)}, f32[10]{0:T(128)}, u32[]{:S(2)}) copy-start(f32[10]{0:T(128)} %param.9) | copy-start | bytes 124
  55.6 27.4 %copy-start.3 = (pred[8]{0:T(512)(128)(4,1)S(1)}, pred[8]{0:T(512)(128)(4,1)}, u32[]{:S(2)}) copy-start(pred[8]{0:T(512)(128)(4,1)} %get-tuple-element.20) | copy-start | bytes 28
  55.6 27.4 %copy-start.4 = (pred[8]{0:T(512)(128)(4,1)S(1)}, pred[8]{0:T(512)(128)(4,1)}, u32[]{:S(2)}) copy-start(pred[8]{0:T(512)(128)(4,1)} %get-tuple-element.21) | copy-start | bytes 28
  55.7 27.4 %copy-start.7 = (pred[8]{0:T(512)(128)(4,1)S(1)}, pred[8]{0:T(512)(128)(4,1)}, u32[]{:S(2)}) copy-start(pred[8]{0:T(512)(128)(4,1)} %get-tuple-element.26) | copy-start | bytes 28
  55.7 27.4 %copy-start.11 = (pred[8]{0:T(512)(128)(4,1)S(1)}, pred[8]{0:T(512)(128)(4,1)}, u32[]{:S(2)}) copy-start(pred[8]{0:T(512)(128)(4,1)} %compare_and_fusion.6) | copy-start | bytes 28
  55.7 27.4 %copy-start.12 = (pred[8]{0:T(512)(128)(4,1)S(1)}, pred[8]{0:T(512)(128)(4,1)}, u32[]{:S(2)}) copy-start(pred[8]{0:T(512)(128)(4,1)} %compare_and_fusion.7) | copy-start | bytes 28
  55.7 27.4 %copy-start.13 = (pred[8]{0:T(512)(128)(4,1)S(1)}, pred[8]{0:T(512)(128)(4,1)}, u32[]{:S(2)}) copy-start(pred[8]{0:T(512)(128)(4,1)} %broadcast_compare_fusion.4) | copy-start | bytes 28
  73.9 23.5 %collective-permute-start.3 = (f32[1,8,16,256]{3,2,1,0:T(8,128)}, f32[1,8,16,256]{3,2,1,0:T(8,128)}, u32[]{:S(2)}, u32[]{:S(2)}) collective-permute-start(f32[1,8,16,256]{3,2,1,0:T(8,128)} %get-tuple-element.63), channel_id=1, source_target_pairs={{4,0},{8,4},{12,8},{5,1},{9,5},{13,9},{6,2},{10,6},{14,10},{7,3},{... | collective-permute-start | bytes 393224 | tf_op jit(solution)/shard_map/ppermute | solution.py:26
  134.9 6.5 %copy-start.9 = (pred[8]{0:T(512)(128)(4,1)S(1)}, pred[8]{0:T(512)(128)(4,1)}, u32[]{:S(2)}) copy-start(pred[8]{0:T(512)(128)(4,1)} %get-tuple-element.121) | copy-start | bytes 28
  134.9 11.9 %copy-start.5 = (pred[8]{0:T(512)(128)(4,1)S(1)}, pred[8]{0:T(512)(128)(4,1)}, u32[]{:S(2)}) copy-start(pred[8]{0:T(512)(128)(4,1)} %get-tuple-element.15) | copy-start | bytes 28
  134.9 11.9 %copy-start.8 = (pred[8]{0:T(512)(128)(4,1)S(1)}, pred[8]{0:T(512)(128)(4,1)}, u32[]{:S(2)}) copy-start(pred[8]{0:T(512)(128)(4,1)} %get-tuple-element.120) | copy-start | bytes 28
  148.5 23.1 %collective-permute-start.8 = (f32[1,8,16,256]{3,2,1,0:T(8,128)}, f32[1,8,16,256]{3,2,1,0:T(8,128)}, u32[]{:S(2)}, u32[]{:S(2)}) collective-permute-start(f32[1,8,16,256]{3,2,1,0:T(8,128)} %get-tuple-element.28), channel_id=1, source_target_pairs={{0,4},{4,8},{8,12},{1,5},{5,9},{9,13},{2,6},{6,10},{10,14},{3,7},{... | collective-permute-start | bytes 393224 | tf_op jit(solution)/shard_map/ppermute | solution.py:24
  153.7 26.6 %collective-permute-start.9 = (f32[1,8,16,256]{3,2,1,0:T(8,128)}, f32[1,8,16,256]{3,2,1,0:T(8,128)}, u32[]{:S(2)}, u32[]{:S(2)}) collective-permute-start(f32[1,8,16,256]{3,2,1,0:T(8,128)} %get-tuple-element.29), channel_id=1, source_target_pairs={{4,0},{8,4},{12,8},{5,1},{9,5},{13,9},{6,2},{10,6},{14,10},{7,3},{... | collective-permute-start | bytes 393224 | tf_op jit(solution)/shard_map/ppermute | solution.py:26
  167.0 15.5 %collective-permute-start.10 = (f32[1,8,16,256]{3,2,1,0:T(8,128)}, f32[1,8,16,256]{3,2,1,0:T(8,128)}, u32[]{:S(2)}, u32[]{:S(2)}) collective-permute-start(f32[1,8,16,256]{3,2,1,0:T(8,128)} %bitcast.199), channel_id=1, source_target_pairs={{0,1},{2,3},{4,5},{6,7},{8,9},{10,11},{12,13},{14,15},{16,17},{18,... | collective-permute-start | bytes 393224 | tf_op jit(solution)/shard_map/ppermute | solution.py:24
  169.0 15.8 %collective-permute-start.11 = (f32[1,8,16,256]{3,2,1,0:T(8,128)}, f32[1,8,16,256]{3,2,1,0:T(8,128)}, u32[]{:S(2)}, u32[]{:S(2)}) collective-permute-start(f32[1,8,16,256]{3,2,1,0:T(8,128)} %bitcast.197), channel_id=1, source_target_pairs={{1,0},{3,2},{5,4},{7,6},{9,8},{11,10},{13,12},{15,14},{17,16},{19,... | collective-permute-start | bytes 393224 | tf_op jit(solution)/shard_map/ppermute | solution.py:26
  170.3 18.4 %collective-permute-start.7 = (f32[1,8,16,256]{3,2,1,0:T(8,128)}, f32[1,8,16,256]{3,2,1,0:T(8,128)}, u32[]{:S(2)}, u32[]{:S(2)}) collective-permute-start(f32[1,8,16,256]{3,2,1,0:T(8,128)} %get-tuple-element.50), channel_id=1, source_target_pairs={{2,0},{3,1},{6,4},{7,5},{10,8},{11,9},{14,12},{15,13},{18,16},{19,... | collective-permute-start | bytes 393224 | tf_op jit(solution)/shard_map/ppermute | solution.py:26
  171.6 21.0 %collective-permute-start.6 = (f32[1,8,16,256]{3,2,1,0:T(8,128)}, f32[1,8,16,256]{3,2,1,0:T(8,128)}, u32[]{:S(2)}, u32[]{:S(2)}) collective-permute-start(f32[1,8,16,256]{3,2,1,0:T(8,128)} %get-tuple-element.51), channel_id=1, source_target_pairs={{0,2},{1,3},{4,6},{5,7},{8,10},{9,11},{12,14},{13,15},{16,18},{17,... | collective-permute-start | bytes 393224 | tf_op jit(solution)/shard_map/ppermute | solution.py:24
  (2 other events, 8.3 us)
where the time goes:
time: 238 us; the launch traced here: 235 us
  local copies, waits for them, and re-layouts  124 us (52%)
  other arithmetic  70.5 us (30%)
  starting transfers between devices  35.6 us (15%)
  between operations  4.44 us (2%)
    gather x24, local copies, waits for them, and re-layouts, select_face(): chosen = jnp.take(table, where_slot[:, column], axis=0)  46.6 us
    ppermute x6, starting transfers between devices, padded(): lax.ppermute(tail, axis, [(i, (i + 1) % count) for i in range(ends)])  27.7 us
    add x1, other arithmetic, on_device(): return initial + 0.5 * (rate_one + rate_two)  17.6 us
    add x1, other arithmetic, on_device(): middle = initial + rate_one  17.1 us
    select_n x8, other arithmetic, select_face(): return jnp.where(present[:, column, None, None], chosen, 0.0)  10.9 us
    ppermute x6, starting transfers between devices, padded(): lax.ppermute(head, axis, [((i + 1) % count, i) for i in range(ends)])  7.87 us
    another operation x4, local copies, waits for them, and re-layouts, generator(): jnp.tile(jnp.swapaxes(face_set[4], 1, 2), (1, 1, tile_edge))  7.47 us
    unnamed x35, local copies, waits for them, and re-layouts  6.76 us
  transfers between devices with their start and end apart: 12, of which 0 were waited for; matrix products, arithmetic and copies ran while one was open for 42% of the time, Pallas kernels for 0%

commit v1 on v0

v1 whole, which is shorter than its diff:
```python
import functools

import jax
import jax.numpy as jnp
from jax import lax
from jax.experimental import pallas as pl
from jax.experimental.pallas import tpu as pltpu
from jax.sharding import PartitionSpec as P

C_DEV = 2
D_DEV = 2
N1 = 512
N2 = 512
N3 = 256
N4 = 256
EDGE = 16
F32 = jnp.float32
MESH = pl.DeviceIdType.MESH

BELOW_ONE, ABOVE_THREE, BELOW_TWO, ABOVE_FOUR, OUT_LANE, LOCAL_ABOVE, LOCAL_BELOW = range(7)
FAR_ABOVE_FOUR, FAR_BELOW_FOUR, FAR_ABOVE_THREE, FAR_BELOW_THREE = range(7, 11)
LANE_ROWS = 11
MAKE_THREE, ABOVE_TWO, OUT_ROW = range(3)
MAKE_FOUR, ABOVE_ONE, OUT_ONE = range(3)


def kernel(counts, x_ref, coord_ref, near_ref, rate_ref, out_ref,
           v, m, y, lane_c, row_c, one_c, pack3, pack4, far1_a, far1_b, far3_a, far3_b, far4_a, far4_b,
           load_sem, store_sem, send1, recv1, send3, recv3, send4, recv4):
    slots = x_ref.shape[0]
    zero_slot = slots
    far1, far3, far4 = (far1_a, far1_b), (far3_a, far3_b), (far4_a, far4_b)
    own_count, sub_count, rep_count = counts
    own = lax.axis_index("own")
    sub = lax.axis_index("sub")
    rep = lax.axis_index("rep")

    loads = [
        pltpu.make_async_copy(x_ref.at[s], v.at[s], load_sem.at[s]) for s in range(slots)
    ]
    for copy in loads:
        copy.start()

    barrier = pltpu.get_barrier_semaphore()
    expected = jnp.int32(0)
    for axis, index, count in (("own", own, own_count), ("sub", sub, sub_count), ("rep", rep, rep_count)):
        for step, there in ((-1, index > 0), (1, index < count - 1)):
            expected = expected + there.astype(jnp.int32)

            @pl.when(there)
            def _():
                pl.semaphore_signal(
                    barrier, inc=1, device_id={axis: index + step}, device_id_type=MESH
                )

    def own_copies(stage, source):
        down = pltpu.make_async_remote_copy(
            src_ref=source.at[pl.ds(0, slots), pl.ds(0, 2)],
            dst_ref=far1[stage].at[1],
            send_sem=send1.at[stage, 0],
            recv_sem=recv1.at[stage, 1],
            device_id={"own": own - 1},
            device_id_type=MESH,
        )
        up = pltpu.make_async_remote_copy(
            src_ref=source.at[pl.ds(0, slots), pl.ds(2 * EDGE - 2, 2)],
            dst_ref=far1[stage].at[0],
            send_sem=send1.at[stage, 1],
            recv_sem=recv1.at[stage, 0],
            device_id={"own": own + 1},
            device_id_type=MESH,
        )
        return (down, own > 0), (up, own < own_count - 1)

    def face_copies(stage, axis, index, count, pack, far, send, recv):
        if count == 2:
            return (
                (
                    pltpu.make_async_remote_copy(
                        src_ref=pack.at[stage, 0],
                        dst_ref=far[stage].at[0],
                        send_sem=send.at[stage, 0],
                        recv_sem=recv.at[stage, 0],
                        device_id={axis: 1 - index},
                        device_id_type=MESH,
                    ),
                    index >= 0,
                ),
            )
        return tuple(
            (
                pltpu.make_async_remote_copy(
                    src_ref=pack.at[stage, side],
                    dst_ref=far[stage].at[1 - side],
                    send_sem=send.at[stage, side],
                    recv_sem=recv.at[stage, 1 - side],
                    device_id={axis: index + 2 * side - 1},
                    device_id_type=MESH,
                ),
                index > 0 if side == 0 else index < count - 1,
            )
            for side in (0, 1)
        )

    def start_all(copies):
        for copy, there in copies:

            @pl.when(there)
            def _():
                copy.start()

    def sub_copies(stage):
        return face_copies(stage, "sub", sub, sub_count, pack3, far3, send3, recv3)

    def rep_copies(stage):
        return face_copies(stage, "rep", rep, rep_count, pack4, far4, send4, recv4)

    def finish(copies):
        for copy, there in copies:

            @pl.when(there)
            def _():
                copy.wait_send()

    def arrivals(copies, flip):
        order = copies[::-1] if flip and len(copies) == 2 else copies
        for (copy, _), (_, there) in zip(order, copies):

            @pl.when(there)
            def _():
                copy.wait_recv()

    lane = lax.broadcasted_iota(jnp.int32, (8, 128), 1)
    sublane = lax.broadcasted_iota(jnp.int32, (8, 128), 0)
    low = lane % EDGE
    rate = [rate_ref[k] for k in range(10)]

    v[zero_slot] = jnp.zeros(v.shape[1:], F32)
    m[zero_slot] = jnp.zeros(m.shape[1:], F32)

    def far_sides(s):
        below_three_far = coord_ref[s, 2] % C_DEV == 0
        below_four_far = coord_ref[s, 3] % D_DEV == 0
        return below_three_far, below_four_far

    def flag(value):
        return jnp.where(value, 1.0, 0.0)

    def coefficients(s, _):
        base = [(coord_ref[s, k] * EDGE).astype(F32) for k in range(4)]
        below_three_far, below_four_far = far_sides(s)
        there = [near_ref[s, k] >= 0 for k in range(8)]
        far_below_three = flag(below_three_far & there[4])
        far_above_three = flag(jnp.logical_not(below_three_far) & there[5])
        far_below_four = flag(below_four_far & there[6])
        far_above_four = flag(jnp.logical_not(below_four_far) & there[7])
        local_below = flag(jnp.logical_not(below_four_far) & there[6])
        local_above = flag(below_four_far & there[7])
        level_four = base[3] + low.astype(F32)
        above_four = rate[6] * ((level_four + 1.0) * (1.0 / N4))
        for h in range(2):
            level_three = base[2] + (lane // EDGE + 8 * h).astype(F32)
            share_three = level_three * (1.0 / N3)
            share_four = level_four * (1.0 / N4)
            above_three = rate[1] * ((level_three + 1.0) * (1.0 / N3))
            cols = pl.ds(128 * h, 128)
            lane_c[s, BELOW_ONE, :, cols] = rate[2] * share_three
            lane_c[s, ABOVE_THREE, :, cols] = above_three
            lane_c[s, BELOW_TWO, :, cols] = rate[7] * share_four
            lane_c[s, ABOVE_FOUR, :, cols] = jnp.where(low == EDGE - 1, 0.0, above_four)
            lane_c[s, OUT_LANE, :, cols] = (
                rate[1] * share_three + rate[2] * share_three
                + rate[6] * share_four + rate[7] * share_four
            )
            lane_c[s, LOCAL_ABOVE, :, cols] = jnp.where(low == EDGE - 1, above_four, 0.0) * local_above
            lane_c[s, LOCAL_BELOW, :, cols] = jnp.where(low == 0, local_below, 0.0)
            lane_c[s, FAR_ABOVE_FOUR, :, cols] = (
                jnp.where(low == EDGE - 1, above_four, 0.0) * far_above_four
            )
            lane_c[s, FAR_BELOW_FOUR, :, cols] = jnp.where(low == 0, far_below_four, 0.0)
            lane_c[s, FAR_ABOVE_THREE, :, cols] = (
                jnp.where(lane >= 128 - EDGE, above_three, 0.0) * far_above_three
            )
            lane_c[s, FAR_BELOW_THREE, :, cols] = jnp.where(lane < EDGE, far_below_three, 0.0)
        for j in range(2):
            level_two = base[1] + (sublane + 8 * j).astype(F32)
            share_two = level_two * (1.0 / N2)
            ratio_two = share_two / rate[4]
            make_three = rate[0] / (1.0 + ratio_two * ratio_two)
            row_c[s, MAKE_THREE, j] = make_three
            row_c[s, ABOVE_TWO, j] = rate[8] * ((level_two + 1.0) * (1.0 / N2))
            row_c[s, OUT_ROW, j] = make_three + rate[8] * share_two

        def by_one(i, _):
            level_one = jnp.full((8, 128), base[0] + i.astype(F32), F32)
            share_one = level_one * (1.0 / N1)
            ratio_one = share_one / rate[9]
            make_four = rate[5] / (1.0 + ratio_one * ratio_one)
            one_c[s, i, MAKE_FOUR] = make_four
            one_c[s, i, ABOVE_ONE] = rate[3] * ((level_one + 1.0) * (1.0 / N1))
            one_c[s, i, OUT_ONE] = make_four + rate[3] * share_one
            return 0

        lax.fori_loop(0, EDGE, by_one, 0)
        return 0

    lax.fori_loop(0, slots, coefficients, 0)

    pl.semaphore_wait(barrier, expected)
    start_all(own_copies(0, x_ref))
    for copy in loads:
        copy.wait()

    def sides_of(index, count):
        return ((0, (index == 0).astype(jnp.int32)),) if count == 2 else ((0, 0), (1, 1))

    def pack_into(stage, rows, gathered):
        for where, side in sides_of(sub, sub_count):
            for j in range(2):
                total = jnp.zeros((8, 128), F32)
                for s in range(slots):
                    cells = jnp.where(side == 1, gathered[s][j][1], gathered[s][j][0])
                    turned = pltpu.roll(cells, (EDGE * s + EDGE * side) % 128, 1)
                    total = jnp.where(lane // EDGE == s, turned, total)
                pack3[stage, where, rows + j] = total
        for where, side in sides_of(rep, rep_count):
            for j in range(2):
                total = jnp.zeros((8, 128), F32)
                for s in range(slots):
                    for h in range(2):
                        turned = pltpu.roll(
                            gathered[s][j][h], (s + 8 * h + 128 - (EDGE - 1) * side) % 128, 1
                        )
                        total = jnp.where(low == s + 8 * h, turned, total)
                pack4[stage, where, rows + j] = total

    def first_pack(i, _):
        rows = 2 * i
        gathered = [
            [[v[s, rows + j, :, pl.ds(128 * h, 128)] for h in range(2)] for j in range(2)]
            for s in range(slots)
        ]
        pack_into(0, rows, gathered)
        return 0

    lax.fori_loop(0, EDGE, first_pack, 0)
    start_all(sub_copies(0))
    start_all(rep_copies(0))

    def local_index(s, k):
        return jnp.where(near_ref[s, k] >= 0, jnp.maximum(near_ref[s, k], 0) % slots, zero_slot)

    def local_pass(src, put):
        def by_slot(s, _):
            below_three_far, below_four_far = far_sides(s)
            two_low = local_index(s, 2)
            two_high = local_index(s, 3)
            three_low = jnp.where(below_three_far, zero_slot, local_index(s, 4))
            three_high = jnp.where(below_three_far, local_index(s, 5), zero_slot)
            four = jnp.where(below_four_far, local_index(s, 7), local_index(s, 6))
            four_turn = jnp.where(below_four_far, EDGE - 1, 128 - (EDGE - 1))

            def by_one(i, _):
                rows = 2 * i
                under = jnp.where(i == 0, zero_slot, s)
                over = jnp.where(i == EDGE - 1, zero_slot, s)
                under_rows = jnp.maximum(rows - 2, 0)
                over_rows = jnp.minimum(rows + 2, 2 * EDGE - 2)
                make_four = one_c[s, i, MAKE_FOUR]
                above_one_c = one_c[s, i, ABOVE_ONE]
                out_one = one_c[s, i, OUT_ONE]
                inner_below = jnp.where(low == 0, 0.0, make_four)
                cells = [
                    [src[s, rows + j, :, pl.ds(128 * h, 128)] for h in range(2)] for j in range(2)
                ]
                for j in range(2):
                    make_three = row_c[s, MAKE_THREE, j]
                    above_two_c = row_c[s, ABOVE_TWO, j]
                    out_row = row_c[s, OUT_ROW, j] + out_one
                    before = src[three_low, rows + j, :, pl.ds(128, 128)]
                    after = src[three_high, rows + j, :, pl.ds(0, 128)]
                    left, right = cells[j]
                    up_edge = lane >= 128 - EDGE
                    down_edge = lane < EDGE
                    below_three = (
                        pltpu.roll(jnp.where(up_edge, before, left), EDGE, 1),
                        pltpu.roll(jnp.where(up_edge, left, right), EDGE, 1),
                    )
                    above_three = (
                        pltpu.roll(jnp.where(down_edge, right, left), 128 - EDGE, 1),
                        pltpu.roll(jnp.where(down_edge, after, right), 128 - EDGE, 1),
                    )
                    for h in range(2):
                        cols = pl.ds(128 * h, 128)
                        here = cells[j][h]
                        if j == 0:
                            lower = src[two_low, rows + 1, :, cols]
                            upper = cells[1][h]
                        else:
                            lower = cells[0][h]
                            upper = src[two_high, rows, :, cols]
                        below_two = pltpu.roll(jnp.where(sublane == 7, lower, here), 1, 0)
                        above_two = pltpu.roll(jnp.where(sublane == 0, upper, here), 7, 0)
                        across = pltpu.roll(src[four, rows + j, :, cols], four_turn, 1)
                        total = make_three * below_three[h]
                        total += lane_c[s, ABOVE_THREE, :, cols] * above_three[h]
                        total += lane_c[s, BELOW_ONE, :, cols] * src[under, under_rows + j, :, cols]
                        total += above_one_c * src[over, over_rows + j, :, cols]
                        total += lane_c[s, BELOW_TWO, :, cols] * below_two
                        total += above_two_c * above_two
                        total += inner_below * pltpu.roll(here, 1, 1)
                        total += lane_c[s, ABOVE_FOUR, :, cols] * pltpu.roll(here, 127, 1)
                        total += (
                            make_four * lane_c[s, LOCAL_BELOW, :, cols]
                            + lane_c[s, LOCAL_ABOVE, :, cols]
                        ) * across
                        total -= (out_row + lane_c[s, OUT_LANE, :, cols]) * here
                        put(s, rows + j, cols, here, total)
                return 0

            lax.fori_loop(0, EDGE, by_one, 0)
            return 0

        lax.fori_loop(0, slots, by_slot, 0)

    def far_turns(s):
        below_three_far, below_four_far = far_sides(s)
        three = jnp.maximum(jnp.where(below_three_far, near_ref[s, 4], near_ref[s, 5]), 0) % slots
        four = jnp.maximum(jnp.where(below_four_far, near_ref[s, 6], near_ref[s, 7]), 0) % slots
        three_turn = (jnp.where(below_three_far, 128, 128 + 128 - EDGE) - EDGE * three) % 128
        four_turn = jnp.where(below_four_far, 128, 128 + EDGE - 1) - four
        three_side = jnp.where(below_three_far, 0, 1) if sub_count > 2 else 0
        four_side = jnp.where(below_four_far, 0, 1) if rep_count > 2 else 0
        return three_side, three_turn, four_side, four_turn % 128, (four_turn - 8) % 128

    def far_terms(stage, s, i, turns):
        three_side, three_turn, four_side, turn_left, turn_right = turns
        rows = 2 * i
        make_four = one_c[s, i, MAKE_FOUR]
        terms = []
        for j in range(2):
            third = pltpu.roll(far3[stage][three_side, rows + j], three_turn, 1)
            fourth = far4[stage][four_side, rows + j]
            halves = []
            for h, turn in ((0, turn_left), (1, turn_right)):
                cols = pl.ds(128 * h, 128)
                weight = (
                    make_four * lane_c[s, FAR_BELOW_FOUR, :, cols]
                    + lane_c[s, FAR_ABOVE_FOUR, :, cols]
                )
                edge = (
                    row_c[s, MAKE_THREE, j] * lane_c[s, FAR_BELOW_THREE, :, cols]
                    if h == 0
                    else lane_c[s, FAR_ABOVE_THREE, :, cols]
                )
                term = jnp.where(edge != 0.0, edge * third, 0.0)
                term += jnp.where(weight != 0.0, weight * pltpu.roll(fourth, turn, 1), 0.0)
                halves.append(term)
            terms.append(halves)
        return terms

    def first_terms(stage, s, cols, j):
        under = jnp.maximum(near_ref[s, 0], 0) % slots
        over = jnp.maximum(near_ref[s, 1], 0) % slots
        below = lane_c[s, BELOW_ONE, :, cols] * far1[stage][0, under, j, :, cols]
        above = one_c[s, EDGE - 1, ABOVE_ONE] * far1[stage][1, over, j, :, cols]
        return (
            jnp.where(near_ref[s, 0] >= 0, below, 0.0),
            jnp.where(near_ref[s, 1] >= 0, above, 0.0),
        )

    def add_first(stage, target, scale):
        def by_slot(s, _):
            for j in range(2):
                for h in range(2):
                    cols = pl.ds(128 * h, 128)
                    below, above = first_terms(stage, s, cols, j)
                    target[s, j, :, cols] += scale * below
                    target[s, 2 * EDGE - 2 + j, :, cols] += scale * above
            return 0

        lax.fori_loop(0, slots, by_slot, 0)

    def put_middle(s, row, cols, here, total):
        m[s, row, :, cols] = here + total

    local_pass(v, put_middle)

    arrivals(own_copies(0, x_ref), True)
    add_first(0, m, 1.0)
    arrivals(sub_copies(0), True)
    arrivals(rep_copies(0), True)

    def second_pack(i, _):
        rows = 2 * i
        gathered = []
        for s in range(slots):
            terms = far_terms(0, s, i, far_turns(s))
            tile = []
            for j in range(2):
                halves = []
                for h in range(2):
                    cols = pl.ds(128 * h, 128)
                    cells = m[s, rows + j, :, cols] + terms[j][h]
                    m[s, rows + j, :, cols] = cells
                    halves.append(cells)
                tile.append(halves)
            gathered.append(tile)
        pack_into(1, rows, gathered)
        return 0

    lax.fori_loop(0, EDGE, second_pack, 0)
    start_all(own_copies(1, m))
    start_all(sub_copies(1))
    start_all(rep_copies(1))

    def put_next(s, row, cols, here, total):
        y[s, row, :, cols] = 0.5 * (v[s, row, :, cols] + here + total)

    local_pass(m, put_next)

    arrivals(own_copies(1, m), True)
    add_first(1, y, 0.5)
    arrivals(sub_copies(1), True)
    arrivals(rep_copies(1), True)

    stores = [
        pltpu.make_async_copy(y.at[s], out_ref.at[s], store_sem.at[s]) for s in range(slots)
    ]
    for s in range(slots):
        turns = far_turns(s)
        active = coord_ref[s, 0] >= 0

        def by_one(i, _):
            rows = 2 * i
            terms = far_terms(1, s, i, turns)
            for j in range(2):
                for h in range(2):
                    cols = pl.ds(128 * h, 128)
                    cells = y[s, rows + j, :, cols] + 0.5 * terms[j][h]
                    y[s, rows + j, :, cols] = jnp.where(active, cells, 0.0)
            return 0

        lax.fori_loop(0, EDGE, by_one, 0)
        stores[s].start()
    for stage, source in ((0, x_ref), (1, m)):
        finish(own_copies(stage, source))
        finish(sub_copies(stage))
        finish(rep_copies(stage))
    for copy in stores:
        copy.wait()


def solution(mesh):
    counts = tuple(mesh.shape[axis] for axis in ("own", "sub", "rep"))

    def on_device(density, tile_coords, neighbours, rate_constants):
        slots, area, _ = density.shape
        cells = density.reshape(slots, area // 8, 8, area)
        tile = (slots + 1, area // 8, 8, area)
        face = (2, 2, area // 8, 8, 128)
        smem = pl.BlockSpec(memory_space=pltpu.SMEM)
        dma = pltpu.SemaphoreType.DMA
        out = pl.pallas_call(
            functools.partial(kernel, counts),
            out_shape=jax.ShapeDtypeStruct(cells.shape, F32),
            in_specs=[pl.BlockSpec(memory_space=pl.ANY), smem, smem, smem],
            out_specs=pl.BlockSpec(memory_space=pl.ANY),
            scratch_shapes=[
                pltpu.VMEM(tile, F32),
                pltpu.VMEM(tile, F32),
                pltpu.VMEM(cells.shape, F32),
                pltpu.VMEM((slots, LANE_ROWS, 8, area), F32),
                pltpu.VMEM((slots, 3, 2, 8, 128), F32),
                pltpu.VMEM((slots, EDGE, 3, 8, 128), F32),
                pltpu.VMEM(face, F32),
                pltpu.VMEM(face, F32),
                *[pltpu.VMEM((2, slots, 2, 8, area), F32)] * 2,
                *[pltpu.VMEM(face[1:], F32)] * 4,
                dma((slots,)),
                dma((slots,)),
                dma((2, 2)),
                dma((2, 2)),
                dma((2, 2)),
                dma((2, 2)),
                dma((2, 2)),
                dma((2, 2)),
            ],
            compiler_params=pltpu.CompilerParams(
                collective_id=0, has_side_effects=True, vmem_limit_bytes=40 << 20
            ),
        )(cells, tile_coords, neighbours, rate_constants)
        return out.reshape(density.shape)

    spec = P(("parts", "own", "sub", "rep"), None)
    cube = P(("parts", "own", "sub", "rep"), None, None)
    return jax.shard_map(
        on_device, mesh=mesh, in_specs=(cube, spec, spec, P("parts")), out_specs=cube, check_vma=False
    )
```

time: 238 us -> 52.6 us (0.22); the launches traced: 235 us -> 52.4 us
  local copies, waits for them, and re-layouts: 124 us -> 5.01 us
  other arithmetic: 70.5 us -> 0 us
  Pallas kernels: 0 us -> 47.4 us
  starting transfers between devices: 35.6 us -> 0 us
  between operations: 4.44 us -> 0.01 us
    pallas_call x0 -> x1, Pallas kernels: none -> 47.4 us  [on_device(): pl.pallas_call(functools.partial(kernel, counts), out_shape=jax.ShapeDtyp...]
    gather x24 -> x0, local copies, waits for them, and re-layouts: 46.6 us -> none  [select_face(): chosen = jnp.take(table, where_slot[:, column], axis=0)]
    ppermute x12 -> x0, starting transfers between devices: 35.6 us -> none  [the longest x6 27.7 us: padded(): lax.ppermute(tail, axis, [(i, (i + 1) % count) for i in range(ends)])]
    add x2 -> x0, other arithmetic: 34.7 us -> none  [the longest x1 17.6 us: on_device(): return initial + 0.5 * (rate_one + rate_two)]
    slice x21 -> x0, local copies, waits for them, and re-layouts: 33.4 us -> none  [the longest x2 4.43 us: generator(): jnp.roll(values, -1, axis=2)]
    another operation x12 -> x0, local copies, waits for them, and re-layouts: 19.4 us -> none  [the longest x4 7.47 us: generator(): jnp.tile(jnp.swapaxes(face_set[4], 1, 2), (1, 1, tile_edge))]
    select_n x16 -> x0, other arithmetic: 12.1 us -> none  [the longest x8 10.9 us: select_face(): return jnp.where(present[:, column, None, None], chosen, 0.0)]
    reshape x4 -> x0, local copies, waits for them, and re-layouts: 9.51 us -> none  [the longest x2 4.77 us: generator(): jnp.repeat(jnp.swapaxes(face_set[7], 1, 2), tile_edge, axis=2)]
  transfers between devices with their start and end apart: 12 -> 0, of which waited for: 0 -> 0; matrix products, arithmetic and copies ran while one was open for 42% -> 0% of each run, Pallas kernels for 0% -> 0%
where the time goes in v1:
time: 52.6 us; the launch traced here: 52.4 us
  Pallas kernels  47.4 us (90%)
  local copies, waits for them, and re-layouts  5.01 us (10%)
    pallas_call x1, Pallas kernels, on_device(): pl.pallas_call(functools.partial(kernel, counts), out_shape=jax.ShapeDtyp...  47.4 us
    unnamed x8, local copies, waits for them, and re-layouts  5.01 us

profile of v1, /device:TPU:0, one launch (start us, length us, event | category | flops | bytes accessed | tf_op | source)
XLA Modules:
  0.0 52.4 jit_solution(1257430694848461574)
XLA Ops:
  0.0 0.8 %copy.5.coord_ref = s32[8,4]{1,0:T(8,128)S(1)} copy(s32[8,4]{0,1:T(4,128)} %param.5) | data formatting | bytes 256 | tf_op args[1]
  0.8 0.0 copy-start
  0.8 1.6 %copy-done = f32[8,256,256]{2,1,0:T(8,128)S(1)} copy-done((f32[8,256,256]{2,1,0:T(8,128)S(1)}, f32[8,256,256]{2,1,0:T(8,128)}, u32[]{:S(2)}) %copy-start) | copy-done | bytes 2097176
  2.3 0.0 copy-start.1
  2.4 0.7 %copy-done.1 = s32[8,8]{1,0:T(8,128)S(1)} copy-done((s32[8,8]{1,0:T(8,128)S(1)}, s32[8,8]{1,0:T(8,128)}, u32[]{:S(2)}) %copy-start.1) | copy-done | bytes 280
  3.0 0.0 copy-start.2
  3.0 0.7 %copy-done.2 = f32[10]{0:T(128)S(1)} copy-done((f32[10]{0:T(128)S(1)}, f32[10]{0:T(128)}, u32[]{:S(2)}) %copy-start.2) | copy-done | bytes 64
  3.7 47.4 %shard_map.46 = f32[8,32,8,256]{3,2,1,0:T(8,128)S(1)} custom-call(f32[8,32,8,256]{3,2,1,0:T(8,128)S(1)} %bitcast.3, s32[8,4]{1,0:T(8,128)S(1)} %copy.5.coord_ref, s32[8,8]{1,0:T(8,128)S(1)} %copy-done.1, f32[10]{0:T(128)S(1)} %copy-done.2), custom_call_target="tpu_custom_call" | custom-call | tf_op jit(solution)/shard_map/pallas_call | solution.py:464
  51.1 1.3 %copy.7 = f32[8,256,256]{2,1,0:T(8,128)} copy(f32[8,256,256]{2,1,0:T(8,128)S(1)} %bitcast.2) | data formatting | bytes 4194304
Async XLA Ops:
  0.8 1.6 %copy-start = (f32[8,256,256]{2,1,0:T(8,128)S(1)}, f32[8,256,256]{2,1,0:T(8,128)}, u32[]{:S(2)}) copy-start(f32[8,256,256]{2,1,0:T(8,128)} %param.4) | copy-start | bytes 6291460
  2.3 0.7 %copy-start.1 = (s32[8,8]{1,0:T(8,128)S(1)}, s32[8,8]{1,0:T(8,128)}, u32[]{:S(2)}) copy-start(s32[8,8]{1,0:T(8,128)} %near_ref.1) | copy-start | bytes 772
  3.0 0.7 %copy-start.2 = (f32[10]{0:T(128)S(1)}, f32[10]{0:T(128)}, u32[]{:S(2)}) copy-start(f32[10]{0:T(128)} %rate_ref.1) | copy-start | bytes 124

commit v2 on v1

--- a/solution.py
+++ b/solution.py
@@ -24,8 +24,8 @@
 MAKE_FOUR, ABOVE_ONE, OUT_ONE = range(3)
 
 
-def kernel(counts, x_ref, coord_ref, near_ref, rate_ref, out_ref,
-           v, m, y, lane_c, row_c, one_c, pack3, pack4, far1_a, far1_b, far3_a, far3_b, far4_a, far4_b,
+def kernel(counts, x_ref, coord_hbm, near_hbm, rate_hbm, out_ref,
+           coord_ref, near_ref, rate_ref, small_sem, v, m, y, lane_c, row_c, one_c, pack3, pack4, far1_a, far1_b, far3_a, far3_b, far4_a, far4_b,
            load_sem, store_sem, send1, recv1, send3, recv3, send4, recv4):
     slots = x_ref.shape[0]
     zero_slot = slots
@@ -39,6 +39,15 @@
         pltpu.make_async_copy(x_ref.at[s], v.at[s], load_sem.at[s]) for s in range(slots)
     ]
     for copy in loads:
+        copy.start()
+
+    small = [
+        pltpu.make_async_copy(source, held, small_sem.at[k])
+        for k, (source, held) in enumerate(
+            ((coord_hbm, coord_ref), (near_hbm, near_ref), (rate_hbm, rate_ref))
+        )
+    ]
+    for copy in small:
         copy.start()
 
     barrier = pltpu.get_barrier_semaphore()
@@ -133,6 +142,8 @@
     lane = lax.broadcasted_iota(jnp.int32, (8, 128), 1)
     sublane = lax.broadcasted_iota(jnp.int32, (8, 128), 0)
     low = lane % EDGE
+    for copy in small:
+        copy.wait()
     rate = [rate_ref[k] for k in range(10)]
 
     v[zero_slot] = jnp.zeros(v.shape[1:], F32)
@@ -318,7 +329,7 @@
                         put(s, rows + j, cols, here, total)
                 return 0
 
-            lax.fori_loop(0, EDGE, by_one, 0)
+            lax.fori_loop(0, EDGE, by_one, 0, unroll=4)
             return 0
 
         lax.fori_loop(0, slots, by_slot, 0)
@@ -441,7 +452,7 @@
                     y[s, rows + j, :, cols] = jnp.where(active, cells, 0.0)
             return 0
 
-        lax.fori_loop(0, EDGE, by_one, 0)
+        lax.fori_loop(0, EDGE, by_one, 0, unroll=8)
         stores[s].start()
     for stage, source in ((0, x_ref), (1, m)):
         finish(own_copies(stage, source))
@@ -459,14 +470,17 @@
         cells = density.reshape(slots, area // 8, 8, area)
         tile = (slots + 1, area // 8, 8, area)
         face = (2, 2, area // 8, 8, 128)
-        smem = pl.BlockSpec(memory_space=pltpu.SMEM)
         dma = pltpu.SemaphoreType.DMA
         out = pl.pallas_call(
             functools.partial(kernel, counts),
             out_shape=jax.ShapeDtypeStruct(cells.shape, F32),
-            in_specs=[pl.BlockSpec(memory_space=pl.ANY), smem, smem, smem],
+            in_specs=[pl.BlockSpec(memory_space=pl.ANY)] * 4,
             out_specs=pl.BlockSpec(memory_space=pl.ANY),
             scratch_shapes=[
+                pltpu.SMEM(tile_coords.shape, jnp.int32),
+                pltpu.SMEM(neighbours.shape, jnp.int32),
+                pltpu.SMEM(rate_constants.shape, F32),
+                dma((3,)),
                 pltpu.VMEM(tile, F32),
                 pltpu.VMEM(tile, F32),
                 pltpu.VMEM(cells.shape, F32),
@@ -487,7 +501,7 @@
                 dma((2, 2)),
             ],
             compiler_params=pltpu.CompilerParams(
-                collective_id=0, has_side_effects=True, vmem_limit_bytes=40 << 20
+                collective_id=0, has_side_effects=True, vmem_limit_bytes=62 << 20
             ),
         )(cells, tile_coords, neighbours, rate_constants)
         return out.reshape(density.shape)

time: 52.6 us -> 30.7 us (0.58)
  Pallas kernels: 47.4 us -> 26.1 us
  local copies, waits for them, and re-layouts: 5.01 us -> 4.39 us
    pallas_call x1, Pallas kernels: 47.4 us -> 26.1 us  [on_device(): pl.pallas_call(functools.partial(kernel, counts), out_shape=jax.ShapeDtyp...]
    unnamed x8 -> x2, local copies, waits for them, and re-layouts: 5.01 us -> 4.39 us
where the time goes in v2:
time: 30.7 us; the launch traced here: 30.5 us
  Pallas kernels  26.1 us (85%)
  local copies, waits for them, and re-layouts  4.39 us (14%)
    pallas_call x1, Pallas kernels, on_device(): pl.pallas_call(functools.partial(kernel, counts), out_shape=jax.ShapeDtyp...  26.1 us
    unnamed x2, local copies, waits for them, and re-layouts  4.39 us

profile of v2, /device:TPU:0, one launch (start us, length us, event | category | flops | bytes accessed | tf_op | source)
XLA Modules:
  0.0 30.5 jit_solution(7908353412297544126)
XLA Ops:
  0.0 1.3 %copy.5.coord_hbm = s32[8,4]{1,0:T(8,128)} copy(s32[8,4]{0,1:T(4,128)} %param.5) | data formatting | bytes 256 | tf_op args[1]
  1.3 26.1 %shard_map.46 = f32[8,32,8,256]{3,2,1,0:T(8,128)} custom-call(f32[8,32,8,256]{3,2,1,0:T(8,128)} %bitcast.3, s32[8,4]{1,0:T(8,128)} %copy.5.coord_hbm, s32[8,8]{1,0:T(8,128)} %near_hbm.1, f32[10]{0:T(128)} %rate_hbm.1), custom_call_target="tpu_custom_call" | custom-call | tf_op jit(solution)/shard_map/pallas_call | solution.py:474
  27.5 3.0 %copy.7 = f32[8,256,256]{2,1,0:T(8,128)} copy(f32[8,256,256]{2,1,0:T(8,128)} %bitcast.2) | data formatting | bytes 4194304

commit v3 on v2

--- a/solution.py
+++ b/solution.py
@@ -16,6 +16,8 @@
 EDGE = 16
 F32 = jnp.float32
 MESH = pl.DeviceIdType.MESH
+PIECES = 4
+PIECE = EDGE // PIECES
 
 BELOW_ONE, ABOVE_THREE, BELOW_TWO, ABOVE_FOUR, OUT_LANE, LOCAL_ABOVE, LOCAL_BELOW = range(7)
 FAR_ABOVE_FOUR, FAR_BELOW_FOUR, FAR_ABOVE_THREE, FAR_BELOW_THREE = range(7, 11)
@@ -24,9 +26,9 @@
 MAKE_FOUR, ABOVE_ONE, OUT_ONE = range(3)
 
 
-def kernel(counts, x_ref, coord_hbm, near_hbm, rate_hbm, out_ref,
-           coord_ref, near_ref, rate_ref, small_sem, v, m, y, lane_c, row_c, one_c, pack3, pack4, far1_a, far1_b, far3_a, far3_b, far4_a, far4_b,
-           load_sem, store_sem, send1, recv1, send3, recv3, send4, recv4):
+def kernel(counts, x_ref, coord_hbm, near_hbm, rate_hbm, y,
+           coord_ref, near_ref, rate_ref, turn_ref, small_sem, v, m, lane_c, row_c, one_c, pack3, pack4, far1_a, far1_b, far3_a, far3_b, far4_a, far4_b,
+           load_sem, send1, recv1, send3, recv3, send4, recv4):
     slots = x_ref.shape[0]
     zero_slot = slots
     far1, far3, far4 = (far1_a, far1_b), (far3_a, far3_b), (far4_a, far4_b)
@@ -49,6 +51,11 @@
     ]
     for copy in small:
         copy.start()
+
+    for count, far in ((sub_count, far3), (rep_count, far4)):
+        if count > 2:
+            for held in far:
+                held[...] = jnp.zeros_like(held)
 
     barrier = pltpu.get_barrier_semaphore()
     expected = jnp.int32(0)
@@ -81,35 +88,25 @@
         )
         return (down, own > 0), (up, own < own_count - 1)
 
-    def face_copies(stage, axis, index, count, pack, far, send, recv):
-        if count == 2:
-            return (
+    def face_copies(stage, axis, index, count, pack, far, send, recv, piece):
+        rows = pl.ds(2 * PIECE * piece, 2 * PIECE)
+        copies = []
+        for side in (0,) if count == 2 else (0, 1):
+            land = 0 if count == 2 else 1 - side
+            copies.append(
                 (
                     pltpu.make_async_remote_copy(
-                        src_ref=pack.at[stage, 0],
-                        dst_ref=far[stage].at[0],
-                        send_sem=send.at[stage, 0],
-                        recv_sem=recv.at[stage, 0],
-                        device_id={axis: 1 - index},
+                        src_ref=pack.at[stage, side, rows],
+                        dst_ref=far[stage].at[land, rows],
+                        send_sem=send.at[stage, side, piece],
+                        recv_sem=recv.at[stage, land, piece],
+                        device_id={axis: 1 - index if count == 2 else index + 2 * side - 1},
                         device_id_type=MESH,
                     ),
-                    index >= 0,
-                ),
+                    index >= 0 if count == 2 else index > 0 if side == 0 else index < count - 1,
+                )
             )
-        return tuple(
-            (
-                pltpu.make_async_remote_copy(
-                    src_ref=pack.at[stage, side],
-                    dst_ref=far[stage].at[1 - side],
-                    send_sem=send.at[stage, side],
-                    recv_sem=recv.at[stage, 1 - side],
-                    device_id={axis: index + 2 * side - 1},
-                    device_id_type=MESH,
-                ),
-                index > 0 if side == 0 else index < count - 1,
-            )
-            for side in (0, 1)
-        )
+        return tuple(copies)
 
     def start_all(copies):
         for copy, there in copies:
@@ -118,11 +115,14 @@
             def _():
                 copy.start()
 
-    def sub_copies(stage):
-        return face_copies(stage, "sub", sub, sub_count, pack3, far3, send3, recv3)
-
-    def rep_copies(stage):
-        return face_copies(stage, "rep", rep, rep_count, pack4, far4, send4, recv4)
+    def sub_copies(stage, piece):
+        return face_copies(stage, "sub", sub, sub_count, pack3, far3, send3, recv3, piece)
+
+    def rep_copies(stage, piece):
+        return face_copies(stage, "rep", rep, rep_count, pack4, far4, send4, recv4, piece)
+
+    def tile_rows(p):
+        return jnp.where(p == 0, 0, jnp.where(p == 1, EDGE - 1, p - 1))
 
     def finish(copies):
         for copy, there in copies:
@@ -150,15 +150,25 @@
     m[zero_slot] = jnp.zeros(m.shape[1:], F32)
 
     def far_sides(s):
-        below_three_far = coord_ref[s, 2] % C_DEV == 0
-        below_four_far = coord_ref[s, 3] % D_DEV == 0
+        below_three_far = coord_ref[2, s] % C_DEV == 0
+        below_four_far = coord_ref[3, s] % D_DEV == 0
         return below_three_far, below_four_far
 
     def flag(value):
         return jnp.where(value, 1.0, 0.0)
 
+    def far_turns(s):
+        below_three_far, below_four_far = far_sides(s)
+        three = jnp.maximum(jnp.where(below_three_far, near_ref[s, 4], near_ref[s, 5]), 0) % slots
+        four = jnp.maximum(jnp.where(below_four_far, near_ref[s, 6], near_ref[s, 7]), 0) % slots
+        three_turn = (jnp.where(below_three_far, 128, 128 + 128 - EDGE) - EDGE * three) % 128
+        four_turn = jnp.where(below_four_far, 128, 128 + EDGE - 1) - four
+        three_side = jnp.where(below_three_far, 0, 1) if sub_count > 2 else 0
+        four_side = jnp.where(below_four_far, 0, 1) if rep_count > 2 else 0
+        return three_side, three_turn, four_side, four_turn % 128, (four_turn - 8) % 128
+
     def coefficients(s, _):
-        base = [(coord_ref[s, k] * EDGE).astype(F32) for k in range(4)]
+        base = [(coord_ref[k, s] * EDGE).astype(F32) for k in range(4)]
         below_three_far, below_four_far = far_sides(s)
         there = [near_ref[s, k] >= 0 for k in range(8)]
         far_below_three = flag(below_three_far & there[4])
@@ -213,6 +223,8 @@
             return 0
 
         lax.fori_loop(0, EDGE, by_one, 0)
+        for k, turn in enumerate(far_turns(s)):
+            turn_ref[s, k] = jnp.int32(turn)
         return 0
 
     lax.fori_loop(0, slots, coefficients, 0)
@@ -245,18 +257,19 @@
                         total = jnp.where(low == s + 8 * h, turned, total)
                 pack4[stage, where, rows + j] = total
 
-    def first_pack(i, _):
-        rows = 2 * i
+    def first_pack(p, _):
+        rows = 2 * tile_rows(p)
         gathered = [
             [[v[s, rows + j, :, pl.ds(128 * h, 128)] for h in range(2)] for j in range(2)]
             for s in range(slots)
         ]
-        pack_into(0, rows, gathered)
+        pack_into(0, 2 * p, gathered)
         return 0
 
-    lax.fori_loop(0, EDGE, first_pack, 0)
-    start_all(sub_copies(0))
-    start_all(rep_copies(0))
+    for piece in range(PIECES):
+        lax.fori_loop(PIECE * piece, PIECE * (piece + 1), first_pack, 0, unroll=2)
+        start_all(sub_copies(0, piece))
+        start_all(rep_copies(0, piece))
 
     def local_index(s, k):
         return jnp.where(near_ref[s, k] >= 0, jnp.maximum(near_ref[s, k], 0) % slots, zero_slot)
@@ -329,31 +342,23 @@
                         put(s, rows + j, cols, here, total)
                 return 0
 
-            lax.fori_loop(0, EDGE, by_one, 0, unroll=4)
+            lax.fori_loop(0, EDGE, by_one, 0, unroll=16)
             return 0
 
         lax.fori_loop(0, slots, by_slot, 0)
 
-    def far_turns(s):
-        below_three_far, below_four_far = far_sides(s)
-        three = jnp.maximum(jnp.where(below_three_far, near_ref[s, 4], near_ref[s, 5]), 0) % slots
-        four = jnp.maximum(jnp.where(below_four_far, near_ref[s, 6], near_ref[s, 7]), 0) % slots
-        three_turn = (jnp.where(below_three_far, 128, 128 + 128 - EDGE) - EDGE * three) % 128
-        four_turn = jnp.where(below_four_far, 128, 128 + EDGE - 1) - four
-        three_side = jnp.where(below_three_far, 0, 1) if sub_count > 2 else 0
-        four_side = jnp.where(below_four_far, 0, 1) if rep_count > 2 else 0
-        return three_side, three_turn, four_side, four_turn % 128, (four_turn - 8) % 128
-
-    def far_terms(stage, s, i, turns):
-        three_side, three_turn, four_side, turn_left, turn_right = turns
-        rows = 2 * i
+    def far_terms(stage, s, p, i):
+        three_side = turn_ref[s, 0] if sub_count > 2 else 0
+        four_side = turn_ref[s, 2] if rep_count > 2 else 0
+        three_turn = turn_ref[s, 1]
+        rows = 2 * p
         make_four = one_c[s, i, MAKE_FOUR]
         terms = []
         for j in range(2):
             third = pltpu.roll(far3[stage][three_side, rows + j], three_turn, 1)
             fourth = far4[stage][four_side, rows + j]
             halves = []
-            for h, turn in ((0, turn_left), (1, turn_right)):
+            for h in range(2):
                 cols = pl.ds(128 * h, 128)
                 weight = (
                     make_four * lane_c[s, FAR_BELOW_FOUR, :, cols]
@@ -364,9 +369,7 @@
                     if h == 0
                     else lane_c[s, FAR_ABOVE_THREE, :, cols]
                 )
-                term = jnp.where(edge != 0.0, edge * third, 0.0)
-                term += jnp.where(weight != 0.0, weight * pltpu.roll(fourth, turn, 1), 0.0)
-                halves.append(term)
+                halves.append(edge * third + weight * pltpu.roll(fourth, turn_ref[s, 3 + h], 1))
             terms.append(halves)
         return terms
 
@@ -399,14 +402,13 @@
 
     arrivals(own_copies(0, x_ref), True)
     add_first(0, m, 1.0)
-    arrivals(sub_copies(0), True)
-    arrivals(rep_copies(0), True)
-
-    def second_pack(i, _):
+
+    def second_pack(p, _):
+        i = tile_rows(p)
         rows = 2 * i
         gathered = []
         for s in range(slots):
-            terms = far_terms(0, s, i, far_turns(s))
+            terms = far_terms(0, s, p, i)
             tile = []
             for j in range(2):
                 halves = []
@@ -417,13 +419,17 @@
                     halves.append(cells)
                 tile.append(halves)
             gathered.append(tile)
-        pack_into(1, rows, gathered)
+        pack_into(1, 2 * p, gathered)
         return 0
 
-    lax.fori_loop(0, EDGE, second_pack, 0)
-    start_all(own_copies(1, m))
-    start_all(sub_copies(1))
-    start_all(rep_copies(1))
+    for piece in range(PIECES):
+        arrivals(sub_copies(0, piece), True)
+        arrivals(rep_copies(0, piece), True)
+        lax.fori_loop(PIECE * piece, PIECE * (piece + 1), second_pack, 0, unroll=2)
+        if piece == 0:
+            start_all(own_copies(1, m))
+        start_all(sub_copies(1, piece))
+        start_all(rep_copies(1, piece))
 
     def put_next(s, row, cols, here, total):
         y[s, row, :, cols] = 0.5 * (v[s, row, :, cols] + here + total)
@@ -432,34 +438,29 @@
 
     arrivals(own_copies(1, m), True)
     add_first(1, y, 0.5)
-    arrivals(sub_copies(1), True)
-    arrivals(rep_copies(1), True)
-
-    stores = [
-        pltpu.make_async_copy(y.at[s], out_ref.at[s], store_sem.at[s]) for s in range(slots)
-    ]
-    for s in range(slots):
-        turns = far_turns(s)
-        active = coord_ref[s, 0] >= 0
-
-        def by_one(i, _):
-            rows = 2 * i
-            terms = far_terms(1, s, i, turns)
+
+    def last_terms(p, _):
+        i = tile_rows(p)
+        rows = 2 * i
+        for s in range(slots):
+            active = coord_ref[0, s] >= 0
+            terms = far_terms(1, s, p, i)
             for j in range(2):
                 for h in range(2):
                     cols = pl.ds(128 * h, 128)
                     cells = y[s, rows + j, :, cols] + 0.5 * terms[j][h]
                     y[s, rows + j, :, cols] = jnp.where(active, cells, 0.0)
-            return 0
-
-        lax.fori_loop(0, EDGE, by_one, 0, unroll=8)
-        stores[s].start()
+        return 0
+
+    for piece in range(PIECES):
+        arrivals(sub_copies(1, piece), True)
+        arrivals(rep_copies(1, piece), True)
+        lax.fori_loop(PIECE * piece, PIECE * (piece + 1), last_terms, 0, unroll=2)
     for stage, source in ((0, x_ref), (1, m)):
         finish(own_copies(stage, source))
-        finish(sub_copies(stage))
-        finish(rep_copies(stage))
-    for copy in stores:
-        copy.wait()
+        for piece in range(PIECES):
+            finish(sub_copies(stage, piece))
+            finish(rep_copies(stage, piece))
 
 
 def solution(mesh):
@@ -475,15 +476,15 @@
             functools.partial(kernel, counts),
             out_shape=jax.ShapeDtypeStruct(cells.shape, F32),
             in_specs=[pl.BlockSpec(memory_space=pl.ANY)] * 4,
-            out_specs=pl.BlockSpec(memory_space=pl.ANY),
+            out_specs=pl.BlockSpec(memory_space=pltpu.VMEM),
             scratch_shapes=[
-                pltpu.SMEM(tile_coords.shape, jnp.int32),
+                pltpu.SMEM(tile_coords.shape[::-1], jnp.int32),
                 pltpu.SMEM(neighbours.shape, jnp.int32),
                 pltpu.SMEM(rate_constants.shape, F32),
+                pltpu.SMEM((slots, 5), jnp.int32),
                 dma((3,)),
                 pltpu.VMEM(tile, F32),
                 pltpu.VMEM(tile, F32),
-                pltpu.VMEM(cells.shape, F32),
                 pltpu.VMEM((slots, LANE_ROWS, 8, area), F32),
                 pltpu.VMEM((slots, 3, 2, 8, 128), F32),
                 pltpu.VMEM((slots, EDGE, 3, 8, 128), F32),
@@ -492,18 +493,17 @@
                 *[pltpu.VMEM((2, slots, 2, 8, area), F32)] * 2,
                 *[pltpu.VMEM(face[1:], F32)] * 4,
                 dma((slots,)),
-                dma((slots,)),
                 dma((2, 2)),
                 dma((2, 2)),
-                dma((2, 2)),
-                dma((2, 2)),
-                dma((2, 2)),
-                dma((2, 2)),
+                dma((2, 2, PIECES)),
+                dma((2, 2, PIECES)),
+                dma((2, 2, PIECES)),
+                dma((2, 2, PIECES)),
             ],
             compiler_params=pltpu.CompilerParams(
                 collective_id=0, has_side_effects=True, vmem_limit_bytes=62 << 20
             ),
-        )(cells, tile_coords, neighbours, rate_constants)
+        )(cells, tile_coords.T, neighbours, rate_constants)
         return out.reshape(density.shape)
 
     spec = P(("parts", "own", "sub", "rep"), None)

time: 30.7 us -> 24.1 us (0.79)
  Pallas kernels: 26.1 us -> 20.9 us
  local copies, waits for them, and re-layouts: 4.39 us -> 3.05 us
    pallas_call x1, Pallas kernels: 26.1 us -> 20.9 us  [on_device(): pl.pallas_call(functools.partial(kernel, counts), out_shape=jax.ShapeDtyp...]
    unnamed x2 -> x1, local copies, waits for them, and re-layouts: 4.39 us -> 3.05 us
where the time goes in v3:
time: 24.1 us; the launch traced here: 24 us
  Pallas kernels  20.9 us (87%)
  local copies, waits for them, and re-layouts  3.05 us (13%)
    pallas_call x1, Pallas kernels, on_device(): pl.pallas_call(functools.partial(kernel, counts), out_shape=jax.ShapeDtyp...  20.9 us
    unnamed x1, local copies, waits for them, and re-layouts  3.05 us

profile of v3, /device:TPU:0, one launch (start us, length us, event | category | flops | bytes accessed | tf_op | source)
XLA Modules:
  0.0 24.0 jit_solution(4484546942623268589)
XLA Ops:
  0.0 20.9 %shard_map.46 = f32[8,32,8,256]{3,2,1,0:T(8,128)} custom-call(f32[8,32,8,256]{3,2,1,0:T(8,128)} %bitcast.4, s32[4,8]{1,0:T(4,128)} %bitcast.5, s32[8,8]{1,0:T(8,128)} %near_hbm.1, f32[10]{0:T(128)} %rate_hbm.1), custom_call_target="tpu_custom_call" | custom-call | tf_op jit(solution)/shard_map/pallas_call | solution.py:475
  20.9 3.0 %copy.6 = f32[8,256,256]{2,1,0:T(8,128)} copy(f32[8,256,256]{2,1,0:T(8,128)} %bitcast.3) | data formatting | bytes 4194304
